TPU v7x, 1024 devices: a whole 4x4x32 slice. The times are simulated.
1024 devices in a mesh: prow: 128 (over x, z_hi, y, core), pcol: 8 (over z_lo).
Axes of the slice: x: 4, y: 4, z: 32 (z_hi: 4, z_lo: 8; z = z_hi * 8 + z_lo), core: 2. Of those that a mesh axis runs over, the one named last changes fastest.
Arguments:
- ainv_sep: bfloat16 [128, 8, 24, 24576], P(None, 'pcol', None, 'prow'), may hold values from -6 to 6
- lower_blocks: bfloat16 [24576, 768], P(('prow', 'pcol')), may hold values from -0.0546875 to 0.0546875
- pattern: int32 [1024, 12], replicated, may hold values from 0 to 1, as said below
- diag_inv: float32 [768, 64], replicated, may hold values from -6 to 6
Outputs:
- offdiag: float32 [24576, 768], P(('prow', 'pcol'))
- diagonal: float32 [768, 64], replicated
Inputs may be any that keep to these rules, and one draw needn't show every extreme that they name: `pattern`: each block row meets between (3) and 6 supernodes, and some block row meets exactly 6.
All inputs are finite; a program needn't handle non-finite values.
Results may differ from a plain program's by a relative error of at most 0.0003.
Values may be sent and summed in bfloat16 or wider, within the bound.
A program may use at most 64 MiB of HBM per device.

v0:
```python
import jax
import jax.numpy as jnp
from jax import lax
from jax.sharding import PartitionSpec as P


def body(ainv_sep, lower_blocks, pattern, diag_inv):
    width = diag_inv.shape[1]
    groups = lower_blocks.shape[1] // width
    block_rows = lower_blocks.shape[0]
    column_count = lax.axis_size("pcol")
    column_index = lax.axis_index("pcol")
    row_index = lax.axis_index("prow")
    sep_local = ainv_sep.reshape(-1, ainv_sep.shape[3])
    own_pattern = lax.dynamic_slice_in_dim(pattern, row_index * column_count + column_index, 1, 0)[
        0
    ]
    keep = jnp.repeat(own_pattern, width)[None, :] != 0
    masked = jnp.where(keep, lower_blocks, jnp.zeros_like(lower_blocks))
    partial_value = lax.dot_general(
        sep_local,
        lax.all_gather(masked, "prow", axis=0, tiled=True),
        (((0,), (0,)), ((), ())),
        preferred_element_type=jnp.float32,
    )
    offdiag = lax.psum_scatter(-partial_value, "pcol", scatter_dimension=0, tiled=True)
    lower_three = masked.astype(jnp.float32).reshape(block_rows, groups, width)
    image_three = offdiag.reshape(block_rows, groups, width)
    share = jnp.einsum("rks,rkt->kst", lower_three, image_three, precision=lax.Precision.HIGHEST)
    summed = lax.psum(share, ("prow", "pcol"))
    diagonal = diag_inv - summed.reshape(groups * width, width)
    return (offdiag, diagonal)


def solution(mesh):
    placed = (P(None, "pcol", None, "prow"), P(("prow", "pcol"), None), P(), P())
    return jax.shard_map(
        body,
        mesh=mesh,
        in_specs=placed,
        out_specs=(P(("prow", "pcol"), None), P()),
        check_vma=False,
    )
```

profile of v0, /device:TPU:1, one launch (start us, length us, event | category | flops | bytes accessed | tf_op | source)
XLA Modules:
  0.0 1155.4 jit_solution(1080114565006216691)
XLA Ops:
  7.2 0.0 all-gather.2.cloned.1.call-start
  7.2 0.9 fusion.4
  8.1 0.1 broadcast_in_dim.14
  8.2 0.1 ne.21
  8.3 1.4 broadcast_select_fusion
  9.7 0.0 all-gather.2.cloned.1.call-update
  9.7 0.0 reduce-scatter.2.cloned.1.call-start
  9.7 2.2 copy.9
  11.9 209.6 %all-gather.2.cloned.1.call-done = bf16[3072,768]{1,0:T(8,128)(2,1)} async-done(((bf16[24,768]{1,0:T(8,128)(2,1)}), bf16[3072,768]{1,0:T(8,128)(2,1)}) %all-gather.2.cloned.1.call-update) | async-done | bytes 4718608 | tf_op jit(solution)/shard_map/all_gather | solution.py:22
  221.5 0.0 copy-start
  221.5 4.3 fusion
  225.9 0.0 copy-start.1
  225.9 0.0 reduce-scatter.2.cloned.1.call-update
  225.9 0.0 all-reduce.2.cloned.1.call-start
  225.9 0.0 copy-done
  225.9 0.1 reshape.28
  226.1 55.7 %reduce-scatter.2.cloned.1.call-done = f32[24,768]{1,0:T(8,128)} async-done(((f32[192,768]{1,0:T(8,128)}), f32[24,768]{1,0:T(8,128)}) %reduce-scatter.2.cloned.1.call-update) | async-done | bytes 73744 | tf_op jit(solution)/shard_map/reduce_scatter | solution.py:26
  281.8 1.0 reshape.29
  282.7 0.4 fusion.1
  283.1 0.8 copy.12
  283.9 0.0 all-reduce.2.cloned.1.call-update
  284.0 863.3 %all-reduce.2.cloned.1.call-done = f32[768,64]{0,1:T(8,128)} async-done(((f32[768,64]{0,1:T(8,128)}), f32[768,64]{0,1:T(8,128)}) %all-reduce.2.cloned.1.call-update) | async-done | bytes 196624 | tf_op jit(solution)/shard_map/psum | solution.py:30
  1147.2 0.0 copy-done.1
  1147.2 1.6 sub.3
Async XLA Ops:
  7.2 214.4 %all-gather.2.cloned.1.call-start = ((), (), s32[]{:S(2)}) async-start(), calls=%async_computation.1 | async-start | bytes 4755456 | tf_op jit(solution)/shard_map/all_gather | solution.py:22
  9.7 272.1 %reduce-scatter.2.cloned.1.call-start = ((), (), s32[]{:S(2)}) async-start(), calls=%async_computation.2 | async-start | bytes 663552 | tf_op jit(solution)/shard_map/reduce_scatter | solution.py:26
  221.5 4.4 copy-start
  225.9 921.4 %copy-start.1 = (f32[768,64]{0,1:T(8,128)S(1)}, f32[768,64]{0,1:T(8,128)}, u32[]{:S(2)}) copy-start(f32[768,64]{0,1:T(8,128)} %param.7) | copy-start | bytes 589828
  225.9 921.3 %all-reduce.2.cloned.1.call-start = ((), (), s32[]{:S(2)}) async-start(), calls=%async_computation.3 | async-start | bytes 393216 | tf_op jit(solution)/shard_map/psum | solution.py:30
Sparse Core Ops, SparseCore 0:
  14.4 207.1 all-gather.1
  226.0 55.7 reduce-scatter.1
  287.8 859.3 all-reduce.1
where the time goes:
time: 1160 us
  waiting for transfers between devices  1130 us (97%)
  between operations  13.8 us (1%)
    psum x1, waiting for transfers between devices, body(): summed = lax.psum(share, ('prow', 'pcol'))  863 us
    all_gather x1, waiting for transfers between devices, body(): lax.all_gather(masked, 'prow', axis=0, tiled=True)  210 us
    reduce_scatter x1, waiting for transfers between devices, body(): lax.psum_scatter(-partial_value, 'pcol', scatter_dimension=0, tiled=True)  55.7 us
  transfers between devices with their start and end apart: 3, of which 3 were waited for; matrix products, arithmetic and copies ran while one was open for 0% of the time, Pallas kernels for 0%

commit v1 on v0

v1 whole, which is shorter than its diff:
```python
import functools

import jax
import jax.numpy as jnp
from jax import lax
from jax.experimental import pallas as pl
from jax.experimental.pallas import tpu as pltpu
from jax.sharding import PartitionSpec as P

MESH = pl.DeviceIdType.MESH
F32, BF16 = jnp.float32, jnp.bfloat16
GROUPS = [[j for j in range(3) if (j <= m if m < 3 else j >= m - 3)] for m in range(6)]


def tile(m):
    return slice(m * 128, (m + 1) * 128)


def prow_of(x, zh, y, c):
    return ((x * 4 + zh) * 4 + y) * 2 + c


def place(i):
    c, a, w, zh = i // 64, (i // 16) % 4, (i // 4) % 4, i % 4
    x = a * (1 - c) + w * c
    y = w * (1 - c) + a * c
    return prow_of(x, zh, y, c)


def slot_rows(pat):
    rows = [pat[k : k + 1, :] for k in range(12)]
    out = [None] * 12
    run = jnp.zeros_like(rows[0])
    for k in range(6):
        run = run + rows[k]
        out[k] = run * rows[k]
    run = jnp.full_like(rows[0], 6.0)
    for k in range(11, 5, -1):
        out[k] = run * rows[k]
        run = run - rows[k]
    return jnp.concatenate(out + [jnp.zeros_like(rows[0])] * 4, axis=0)


def kernel(
    pat_ref, low_ref, dinv_ref, g_ref, off_ref, diag_ref,
    cb, dd, cp, gv, gt, tm, tp, ee, mp, pt, rr, rl, sh, b1, b2, b3, b4, b5, b6,
    gsem, sa, ra, sb, rb, sc, rc, sd, rd, sp, rp, s_r, r_r, s_l, r_l,
    s1, r1, s2, r2, s3, r3, s4, r4, s5, r5, s6, r6,
):
    p = lax.axis_index("prow")
    zl = lax.axis_index("pcol")
    c, y, zh, x = p % 2, (p // 2) % 4, (p // 8) % 4, p // 32
    w = y * (1 - c) + x * c
    a = x * (1 - c) + y * c

    def send(src, dst, ssem, rsem, prow, pcol):
        return pltpu.make_async_remote_copy(
            src_ref=src, dst_ref=dst, send_sem=ssem, recv_sem=rsem,
            device_id=(prow, pcol), device_id_type=MESH,
        )

    def at_zh(k):
        return prow_of(x, (zh + k) % 4, y, c)

    def at_x(k):
        return prow_of((x + k) % 4, zh, y, c)

    def at_w(k):
        v = (w + k) % 4
        return prow_of(x * (1 - c) + v * c, zh, v * (1 - c) + y * c, c)

    def at_a(k):
        v = (a + k) % 4
        return prow_of(v * (1 - c) + x * c, zh, y * (1 - c) + v * c, c)

    core_peer = prow_of(x, zh, y, 1 - c)
    me8 = y * 2 + c

    def at_8(k):
        v = (me8 + k) % 8
        return prow_of(x, zh, v // 2, v % 2)

    g_copy = pltpu.make_async_copy(g_ref, gv, gsem)
    g_copy.start()

    barrier = pltpu.get_barrier_semaphore()
    for k in range(1, 4):
        pl.semaphore_signal(barrier, inc=1, device_id=(at_zh(k), zl), device_id_type=MESH)
        pl.semaphore_signal(barrier, inc=1, device_id=(at_x(k), zl), device_id_type=MESH)
    for k in range(1, 8):
        pl.semaphore_signal(barrier, inc=1, device_id=(at_8(k), zl), device_id_type=MESH)
        pl.semaphore_signal(barrier, inc=1, device_id=(p, (zl + k) % 8), device_id_type=MESH)

    slots = slot_rows(pat_ref[...].astype(F32)).astype(BF16)
    row = lax.broadcasted_iota(jnp.int32, (144, 1024), 0)
    lane = lax.broadcasted_iota(jnp.int32, (144, 1024), 1)
    wanted = jnp.where(row < 128, place(row % 128) * 8 + zl, p * 8 + row % 8)
    pick = jnp.where(lane == wanted, 1.0, 0.0).astype(BF16)
    table = lax.dot_general(pick, slots, (((1,), (1,)), ((), ())), preferred_element_type=F32)
    low_half = lax.broadcasted_iota(jnp.int32, (144, 128), 1) < 64
    for m in range(6):
        t = jnp.where(low_half, table[:, 2 * m : 2 * m + 1], table[:, 2 * m + 1 : 2 * m + 2])
        tm[:, tile(m)] = t[:128].astype(BF16)
        for q in range(8):
            tp[q, :, tile(m)] = t[128 + q : 129 + q]

    half24 = lax.broadcasted_iota(jnp.int32, (24, 128), 1) < 64
    own = cb.at[w * 4 + zh]
    mine = tp[zl]
    parts = [None] * 3
    for m in range(6):
        val = low_ref[:, tile(m)].astype(F32)
        t = jnp.broadcast_to(mine[:, tile(m)], (24, 128))
        val_r, t_r = pltpu.roll(val, 64, 1), pltpu.roll(t, 64, 1)
        for j in GROUPS[m]:
            goal = jnp.where(half24, 2.0 * j + 1.0, 2.0 * j + 2.0)
            got = jnp.where(t == goal, val, 0.0) + jnp.where(t_r == goal, val_r, 0.0)
            parts[j] = got if parts[j] is None else parts[j] + got
    for j in range(3):
        own[:, tile(j)] = parts[j].astype(BF16)
        cp[zl, :, tile(j)] = parts[j].astype(BF16)

    pl.semaphore_wait(barrier, 20)

    to_zh = [send(own, own, sa.at[k - 1], ra.at[zh], at_zh(k), zl) for k in range(1, 4)]
    for copy in to_zh:
        copy.start()

    def forward(v):
        ref = cb.at[w * 4 + v]
        return [send(ref, ref, sb.at[v, k - 1], rb.at[w * 4 + v], at_w(k), zl) for k in range(1, 4)]

    for copy in forward(zh):
        copy.start()

    gi = lax.broadcasted_iota(jnp.int32, (128, 128), 0)
    gj = lax.broadcasted_iota(jnp.int32, (128, 128), 1)
    perm = jnp.where(gi == place(gj), -1.0, 0.0).astype(BF16)
    oi = lax.broadcasted_iota(jnp.int32, (384, 384), 0)
    oj = lax.broadcasted_iota(jnp.int32, (384, 384), 1)
    order = jnp.where(oj == (oi % 16) * 24 + oi // 16, 1.0, 0.0).astype(BF16)

    for k in (1, 3, 2):
        v = (zh + k) % 4
        ref = cb.at[w * 4 + v]
        send(ref, ref, sa.at[k - 1], ra.at[v], at_zh(k), zl).wait_recv()
        for copy in forward(v):
            copy.start()

    to_zl = [
        send(cp.at[zl], cp.at[zl], sp.at[k], rp.at[zl], p, (zl + k) % 8) for k in range(1, 8)
    ]
    for copy in to_zl:
        copy.start()

    g_copy.wait()

    @pl.loop(0, 24)
    def _(r):
        gt[:, pl.ds(pl.multiple_of(r * 128, 128), 128)] = jnp.dot(
            gv[r], perm, preferred_element_type=F32
        ).astype(BF16)

    for k in (1, 3, 2):
        for v in range(4):
            slot = ((w + k) % 4) * 4 + v
            ref = cb.at[slot]
            send(ref, ref, sb.at[v, k - 1], rb.at[slot], at_w(k), zl).wait_recv()

    group = cb[...].astype(F32).reshape(384, 384).astype(BF16)
    group = jnp.dot(order, group, preferred_element_type=F32)
    dd[c * 4 + a] = group.reshape(24, 16, 384).astype(BF16)

    mine_d = dd.at[c * 4 + a]
    to_a = [send(mine_d, mine_d, sc.at[k - 1], rc.at[a], at_a(k), zl) for k in range(1, 4)]
    for copy in to_a:
        copy.start()

    def to_core(v):
        ref = dd.at[c * 4 + v]
        return send(ref, ref, sd.at[v], rd.at[v], core_peer, zl)

    to_core(a).start()

    half16 = lax.broadcasted_iota(jnp.int32, (16, 128), 1) < 64
    plain = [jnp.where(half16, 2.0 * j + 1.0, 2.0 * j + 2.0).astype(BF16) for j in range(3)]
    swapped = [jnp.where(half16, 2.0 * j + 2.0, 2.0 * j + 1.0).astype(BF16) for j in range(3)]

    def expand(g):
        start = pl.multiple_of(g * 16, 16)

        @pl.loop(0, 24)
        def _(r):
            val = [dd[g, r, :, tile(j)] for j in range(3)]
            val_r = [pltpu.roll(v.astype(F32), 64, 1).astype(BF16) for v in val]
            for m in range(6):
                t = tm[pl.ds(start, 16), tile(m)]
                acc = jnp.zeros((16, 128), BF16)
                for j in GROUPS[m]:
                    acc = jnp.where(t == plain[j], val[j], acc)
                    acc = jnp.where(t == swapped[j], val_r[j], acc)
                ee[pl.ds(pl.multiple_of(r * 128 + g * 16, 16), 16), tile(m)] = acc

    expand(c * 4 + a)

    for k in range(1, 8):
        v = (zl + k) % 8
        send(cp.at[v], cp.at[v], sp.at[k], rp.at[v], p, v).wait_recv()
    goal_p = [jnp.where(half24, 2.0 * j + 1.0, 2.0 * j + 2.0) for j in range(3)]
    goal_s = [jnp.where(half24, 2.0 * j + 2.0, 2.0 * j + 1.0) for j in range(3)]

    @pl.loop(0, 8)
    def _(q):
        val = [cp[q, :, tile(j)].astype(F32) for j in range(3)]
        val_r = [pltpu.roll(v, 64, 1) for v in val]
        for m in range(6):
            t = jnp.broadcast_to(tp[q, :, tile(m)], (24, 128))
            acc = jnp.zeros((24, 128), F32)
            for j in GROUPS[m]:
                acc = jnp.where(t == goal_p[j], val[j], acc)
                acc = jnp.where(t == goal_s[j], val_r[j], acc)
            mp[q, :, tile(m)] = acc

    other = y * (1 - c) + x * c

    def from_core(v):
        ref = dd.at[(1 - c) * 4 + v]
        send(ref, ref, sd.at[v], rd.at[v], core_peer, zl).wait_recv()
        expand((1 - c) * 4 + v)

    from_core(other)
    for k in (1, 3, 2):
        v = (a + k) % 4
        ref = dd.at[c * 4 + v]
        send(ref, ref, sc.at[k - 1], rc.at[v], at_a(k), zl).wait_recv()
        to_core(v).start()
        expand(c * 4 + v)
    for k in (1, 3, 2):
        from_core((other + k) % 4)

    @pl.loop(0, 3)
    def _(n):
        cols = pl.ds(pl.multiple_of(n * 256, 256), 256)
        got = jnp.dot(gt[...], ee[:, cols], preferred_element_type=F32)
        pt[:, :, cols] = got.reshape(8, 24, 256)

    def step_right(j):
        @pl.when(j > zl)
        def _():
            copy = send(rr.at[j], rr.at[j], s_r.at[j], r_r.at[j], p, (zl + 1) % 8)

            @pl.when(zl > 0)
            def _():
                copy.wait_recv()
                rr[j] = rr[j] + pt[j]

            @pl.when(zl == 0)
            def _():
                rr[j] = pt[j]

            if j <= 5:
                nxt = j + 2
                send(rr.at[nxt], rr.at[nxt], s_r.at[nxt], r_r.at[nxt], p, (zl + 1) % 8).wait_send()
            copy.start()

    def step_left(j):
        @pl.when(j < zl)
        def _():
            copy = send(rl.at[j], rl.at[j], s_l.at[j], r_l.at[j], p, (zl + 7) % 8)

            @pl.when(zl < 7)
            def _():
                copy.wait_recv()
                rl[j] = rl[j] + pt[j]

            @pl.when(zl == 7)
            def _():
                rl[j] = pt[j]

            if j >= 2:
                nxt = j - 2
                send(rl.at[nxt], rl.at[nxt], s_l.at[nxt], r_l.at[nxt], p, (zl + 7) % 8).wait_send()
            copy.start()

    step_right(7)
    step_left(0)

    half64 = lax.broadcasted_iota(jnp.int32, (64, 128), 1) < 64
    for m in range(6):
        part = pt[:, :, tile(m)].reshape(192, 128)
        fac = mp[:, :, tile(m)].reshape(192, 128).astype(BF16)
        hi = part.astype(BF16)
        lo = (part - hi.astype(F32)).astype(BF16)
        dims = (((0,), (0,)), ((), ()))
        both = lax.dot_general(hi, fac, dims, preferred_element_type=F32)
        both = both + lax.dot_general(lo, fac, dims, preferred_element_type=F32)
        sh[:, :, tile(m)] = jnp.where(half64, both[:64], both[64:]).reshape(8, 8, 128)

    b1[me8] = sh[me8]
    to_1 = []
    for k in range(1, 8):
        v = (me8 + k) % 8
        to_1.append(send(sh.at[v], b1.at[me8], s1.at[k], r1.at[me8], at_8(k), zl))
    for copy in to_1:
        copy.start()

    def phase1():
        for k in range(1, 8):
            v = (me8 + k) % 8
            send(sh.at[v], b1.at[v], s1.at[k], r1.at[v], at_8(k), zl).wait_recv()
        b2[x] = functools.reduce(lambda u, v: u + v, [b1[v] for v in range(8)])
        for k in range(1, 4):
            send(b2.at[x], b2.at[x], s2.at[k], r2.at[x], at_x(k), zl).start()

    xx = x - x // 3
    cols = pl.ds(pl.multiple_of(xx * 256, 256), 256)

    def phase2():
        for k in range(1, 4):
            v = (x + k) % 4
            send(b2.at[v], b2.at[v], s2.at[k], r2.at[v], at_x(k), zl).wait_recv()
        b3[zl] = functools.reduce(lambda u, v: u + v, [b2[v, :, cols] for v in range(4)])
        for k in range(1, 8):
            send(b3.at[zl], b3.at[zl], s3.at[k], r3.at[zl], p, (zl + k) % 8).start()

    def phase3():
        for k in range(1, 8):
            v = (zl + k) % 8
            send(b3.at[v], b3.at[v], s3.at[k], r3.at[v], p, v).wait_recv()
        b4[zh] = functools.reduce(lambda u, v: u + v, [b3[v] for v in range(8)])
        for k in range(1, 4):
            send(b4.at[zh], b4.at[zh], s4.at[k], r4.at[zh], at_zh(k), zl).start()

    def phase4():
        for k in range(1, 4):
            v = (zh + k) % 4
            send(b4.at[v], b4.at[v], s4.at[k], r4.at[v], at_zh(k), zl).wait_recv()
        b5[x] = functools.reduce(lambda u, v: u + v, [b4[v] for v in range(4)])
        for k in range(1, 4):
            send(b5.at[x], b5.at[x], s5.at[k], r5.at[x], at_x(k), zl).start()

    def phase5():
        for k in range(1, 4):
            v = (x + k) % 4
            send(b5.at[v], b5.at[v], s5.at[k], r5.at[v], at_x(k), zl).wait_recv()
        for v in range(3):
            b6[me8, :, v * 256 : (v + 1) * 256] = b5[v]
        for k in range(1, 8):
            send(b6.at[me8], b6.at[me8], s6.at[k], r6.at[me8], at_8(k), zl).start()

    def phase6():
        for k in range(1, 8):
            v = (me8 + k) % 8
            send(b6.at[v], b6.at[v], s6.at[k], r6.at[v], at_8(k), zl).wait_recv()
        diag_ref[...] = dinv_ref[...] - b6[...].reshape(64, 768)

    phases = [phase1, phase2, phase3, phase4, phase5, phase6]
    for t in range(1, 7):
        step_right(7 - t)
        step_left(t)

    off_ref[...] = pt[zl]

    @pl.when(zl > 0)
    def _():
        send(rr.at[zl], rr.at[zl], s_r.at[zl], r_r.at[zl], p, (zl + 1) % 8).wait_recv()
        off_ref[...] += rr[zl]

    @pl.when(zl < 7)
    def _():
        send(rl.at[zl], rl.at[zl], s_l.at[zl], r_l.at[zl], p, (zl + 7) % 8).wait_recv()
        off_ref[...] += rl[zl]

    for phase in phases:
        phase()

    for copy in to_zh + to_zl + to_a + to_1:
        copy.wait_send()
    for v in range(4):
        for copy in forward(v):
            copy.wait_send()
        to_core(v).wait_send()
    for j in range(1, 8):

        @pl.when(jnp.logical_and(j > zl, j <= zl + 2))
        def _():
            send(rr.at[j], rr.at[j], s_r.at[j], r_r.at[j], p, (zl + 1) % 8).wait_send()

    for j in range(7):

        @pl.when(jnp.logical_and(j < zl, j >= zl - 2))
        def _():
            send(rl.at[j], rl.at[j], s_l.at[j], r_l.at[j], p, (zl + 7) % 8).wait_send()

    for k in range(1, 4):
        send(b2.at[x], b2.at[x], s2.at[k], r2.at[x], at_x(k), zl).wait_send()
        send(b4.at[zh], b4.at[zh], s4.at[k], r4.at[zh], at_zh(k), zl).wait_send()
        send(b5.at[x], b5.at[x], s5.at[k], r5.at[x], at_x(k), zl).wait_send()
    for k in range(1, 8):
        send(b3.at[zl], b3.at[zl], s3.at[k], r3.at[zl], p, (zl + k) % 8).wait_send()
        send(b6.at[me8], b6.at[me8], s6.at[k], r6.at[me8], at_8(k), zl).wait_send()


def body(ainv_sep, lower_blocks, pattern, diag_inv):
    dma = pltpu.SemaphoreType.DMA
    vmem = pltpu.VMEM
    off, diag = pl.pallas_call(
        kernel,
        out_shape=(
            jax.ShapeDtypeStruct((24, 768), F32),
            jax.ShapeDtypeStruct((64, 768), F32),
        ),
        in_specs=[pl.BlockSpec(memory_space=vmem)] * 3 + [pl.BlockSpec(memory_space=pl.ANY)],
        out_specs=(pl.BlockSpec(memory_space=vmem), pl.BlockSpec(memory_space=vmem)),
        scratch_shapes=[
            vmem((16, 24, 384), BF16),
            vmem((8, 24, 16, 384), BF16),
            vmem((8, 24, 384), BF16),
            vmem((24, 192, 128), BF16),
            vmem((192, 3072), BF16),
            vmem((128, 768), BF16),
            vmem((8, 1, 768), F32),
            vmem((3072, 768), BF16),
            vmem((8, 24, 768), F32),
            vmem((8, 24, 768), F32),
            vmem((8, 24, 768), F32),
            vmem((8, 24, 768), F32),
            vmem((8, 8, 768), F32),
            vmem((8, 8, 768), F32),
            vmem((4, 8, 768), F32),
            vmem((8, 8, 256), F32),
            vmem((4, 8, 256), F32),
            vmem((4, 8, 256), F32),
            vmem((8, 8, 768), F32),
            dma,
            dma((3,)), dma((4,)),
            dma((4, 3)), dma((16,)),
            dma((3,)), dma((4,)),
            dma((4,)), dma((4,)),
            dma((8,)), dma((8,)),
            dma((8,)), dma((8,)),
            dma((8,)), dma((8,)),
            dma((8,)), dma((8,)),
            dma((4,)), dma((4,)),
            dma((8,)), dma((8,)),
            dma((4,)), dma((4,)),
            dma((4,)), dma((4,)),
            dma((8,)), dma((8,)),
        ],
        compiler_params=pltpu.CompilerParams(
            collective_id=0, has_side_effects=True, vmem_limit_bytes=48 * 1024 * 1024
        ),
    )(
        pattern.T,
        lower_blocks,
        diag_inv.T,
        ainv_sep.transpose(1, 2, 3, 0).reshape(24, 192, 128),
    )
    return off, diag.T


def solution(mesh):
    return jax.shard_map(
        body,
        mesh=mesh,
        in_specs=(P(None, "pcol", None, "prow"), P(("prow", "pcol"), None), P(), P()),
        out_specs=(P(("prow", "pcol"), None), P()),
        check_vma=False,
    )
```

time: 1160 us -> 188 us (0.16)
  waiting for transfers between devices: 1130 us -> 0 us
  Pallas kernels: 0 us -> 182 us
  between operations: 13.8 us -> 0.65 us
    psum x1 -> x0, waiting for transfers between devices: 863 us -> none  [body(): summed = lax.psum(share, ('prow', 'pcol'))]
    all_gather x1 -> x0, waiting for transfers between devices: 210 us -> none  [body(): lax.all_gather(masked, 'prow', axis=0, tiled=True)]
    pallas_call x0 -> x1, Pallas kernels: none -> 182 us  [body(): pl.pallas_call(kernel, out_shape=(jax.ShapeDtypeStruct((24, 768), F32), j...]
    reduce_scatter x1 -> x0, waiting for transfers between devices: 55.7 us -> none  [body(): lax.psum_scatter(-partial_value, 'pcol', scatter_dimension=0, tiled=True)]
  transfers between devices with their start and end apart: 3 -> 0, of which waited for: 3 -> 0; matrix products, arithmetic and copies ran while one was open for 0% -> 0% of each run, Pallas kernels for 0% -> 0%
where the time goes in v1:
time: 188 us
  Pallas kernels  182 us (97%)
  local copies, waits for them, and re-layouts  5.11 us (3%)
    pallas_call x1, Pallas kernels, body(): pl.pallas_call(kernel, out_shape=(jax.ShapeDtypeStruct((24, 768), F32), j...  182 us
    unnamed x10, local copies, waits for them, and re-layouts  5.11 us

profile of v1, /device:TPU:1, one launch (start us, length us, event | category | flops | bytes accessed | tf_op | source)
XLA Modules:
  0.0 188.1 jit_solution(4075689273737621501)
XLA Ops:
  0.6 0.0 copy-start
  0.6 1.3 copy-done
  1.9 0.0 copy-start.1
  1.9 0.9 copy-done.1
  2.8 0.0 copy-start.2
  2.8 0.8 copy-done.2
  3.7 0.0 copy-start.3
  3.7 0.8 copy-done.3
  4.4 182.3 %shard_map.59 = (f32[24,768]{1,0:T(8,128)S(1)}, f32[64,768]{1,0:T(8,128)S(1)}) custom-call(s32[12,1024]{1,0:T(8,128)S(1)} %bitcast.9, bf16[24,768]{1,0:T(8,128)(2,1)S(1)} %copy-done.3, f32[64,768]{1,0:T(8,128)S(1)} %bitcast.8, bf16[24,192,128]{2,1,0:T(8,128)(2,1)S(1)} %bitcast.6), custom_call_target="tpu_custom_call" | custom-call | tf_op jit(solution)/shard_map/pallas_call | solution.py:407
  186.8 0.6 copy.8
  187.4 0.7 copy.9
Async XLA Ops:
  0.6 1.3 copy-start
  1.9 0.9 copy-start.1
  2.8 0.8 copy-start.2
  3.7 0.8 copy-start.3

commit v2 on v1

v2 whole, which is shorter than its diff:
```python
import functools

import jax
import jax.numpy as jnp
from jax import lax
from jax.experimental import pallas as pl
from jax.experimental.pallas import tpu as pltpu
from jax.sharding import PartitionSpec as P

MESH = pl.DeviceIdType.MESH
F32, BF16 = jnp.float32, jnp.bfloat16
GROUPS = [[j for j in range(3) if (j <= m if m < 3 else j >= m - 3)] for m in range(6)]


def tile(m):
    return slice(m * 128, (m + 1) * 128)


def prow_of(x, zh, y, c):
    return ((x * 4 + zh) * 4 + y) * 2 + c


def place(i):
    c, a, w, zh = i >> 6, (i >> 4) & 3, (i >> 2) & 3, i & 3
    x = jnp.where(c == 0, a, w)
    y = jnp.where(c == 0, w, a)
    return (x << 5) + (zh << 3) + (y << 1) + c


def slot_rows(pat):
    rows = [pat[k : k + 1, :] for k in range(12)]
    out = [None] * 12
    run = jnp.zeros_like(rows[0])
    for k in range(6):
        run = run + rows[k]
        out[k] = run * rows[k]
    run = jnp.full_like(rows[0], 6.0)
    for k in range(11, 5, -1):
        out[k] = run * rows[k]
        run = run - rows[k]
    return jnp.concatenate(out + [jnp.zeros_like(rows[0])] * 4, axis=0)


def kernel(
    pat_hbm, low_hbm, dinv_hbm, g_hbm, off_ref, diag_ref,
    pat_ref, low_ref, dinv_ref, cb, dd, cp, gv, gt, tm, tp, ee, mp, ft, pt, rr, rl, sh, b1, b3, b4, b6,
    isem, sa, ra, sb, rb, sc, rc, sd, rd, sp, rp, s_r, r_r, s_l, r_l,
    s1, r1, s3, r3, s4, r4, s6, r6,
):
    p = lax.axis_index("prow")
    zl = lax.axis_index("pcol")
    c, y, zh, x = p % 2, (p // 2) % 4, (p // 8) % 4, p // 32
    w = y * (1 - c) + x * c
    a = x * (1 - c) + y * c

    def send(src, dst, ssem, rsem, prow, pcol):
        return pltpu.make_async_remote_copy(
            src_ref=src, dst_ref=dst, send_sem=ssem, recv_sem=rsem,
            device_id=(prow, pcol), device_id_type=MESH,
        )

    def at_zh(k):
        return prow_of(x, (zh + k) % 4, y, c)

    def at_w(k):
        v = (w + k) % 4
        return prow_of(x * (1 - c) + v * c, zh, v * (1 - c) + y * c, c)

    def at_a(k):
        v = (a + k) % 4
        return prow_of(v * (1 - c) + x * c, zh, y * (1 - c) + v * c, c)

    core_peer = prow_of(x, zh, y, 1 - c)
    d = (x * 4 + y) * 2 + c

    def in_plane(v):
        return prow_of((v // 8) % 4, zh, (v // 2) % 4, v % 2)


    barrier = pltpu.get_barrier_semaphore()
    for k in (1, 3):
        pl.semaphore_signal(barrier, inc=1, device_id=(at_zh(k), zl), device_id_type=MESH)
    for k in range(1, 8):
        pl.semaphore_signal(barrier, inc=1, device_id=(p, (zl + k) % 8), device_id_type=MESH)
    for k in range(1, 32):
        pl.semaphore_signal(barrier, inc=1, device_id=(in_plane(d + k), zl), device_id_type=MESH)

    pairs = [(pat_hbm, pat_ref), (low_hbm, low_ref), (g_hbm, gv), (dinv_hbm, dinv_ref)]
    loads = [pltpu.make_async_copy(u, v, isem.at[k]) for k, (u, v) in enumerate(pairs)]
    for copy in loads:
        copy.start()
    loads[0].wait()
    loads[1].wait()

    slots = slot_rows(pat_ref[...].astype(F32)).astype(BF16)
    row = lax.broadcasted_iota(jnp.int32, (144, 128), 0)
    lane = lax.broadcasted_iota(jnp.int32, (144, 128), 1)
    wanted = jnp.where(row < 128, (place(row & 127) << 3) + zl, p * 8 + (row & 7)) - lane
    pick = [jnp.where(wanted == 128 * k, 1.0, 0.0).astype(BF16) for k in range(8)]
    pick = jnp.concatenate(pick, axis=1)
    table = lax.dot_general(pick, slots, (((1,), (1,)), ((), ())), preferred_element_type=F32)
    low_half = lane < 64
    for m in range(6):
        t = jnp.where(low_half, table[:, 2 * m : 2 * m + 1], table[:, 2 * m + 1 : 2 * m + 2])
        tm[:, tile(m)] = t[:128].astype(BF16)
        for q in range(8):
            tp[q, :, tile(m)] = t[128 + q : 129 + q]

    half24 = lax.broadcasted_iota(jnp.int32, (24, 128), 1) < 64
    own = cb.at[w * 4 + zh]
    mine = tp[zl]
    parts = [None] * 3
    for m in range(6):
        val = low_ref[:, tile(m)].astype(F32)
        t = jnp.broadcast_to(mine[:, tile(m)], (24, 128))
        val_r, t_r = pltpu.roll(val, 64, 1), pltpu.roll(t, 64, 1)
        for j in GROUPS[m]:
            goal = jnp.where(half24, 2.0 * j + 1.0, 2.0 * j + 2.0)
            got = jnp.where(t == goal, val, 0.0) + jnp.where(t_r == goal, val_r, 0.0)
            parts[j] = got if parts[j] is None else parts[j] + got
    for j in range(3):
        own[:, tile(j)] = parts[j].astype(BF16)
        cp[zl, :, tile(j)] = parts[j].astype(BF16)

    pl.semaphore_wait(barrier, 40)

    to_zh = [send(own, own, sa.at[k // 2], ra.at[zh], at_zh(k), zl) for k in (1, 3)]
    for copy in to_zh:
        copy.start()

    def forward(v):
        ref = cb.at[w * 4 + v]
        return [send(ref, ref, sb.at[v, k - 1], rb.at[w * 4 + v], at_w(k), zl) for k in range(1, 4)]

    for copy in forward(zh):
        copy.start()

    gi = lax.broadcasted_iota(jnp.int32, (128, 128), 0)
    gj = lax.broadcasted_iota(jnp.int32, (128, 128), 1)
    perm = jnp.where(gi == place(gj), -1.0, 0.0).astype(BF16)
    oi = lax.broadcasted_iota(jnp.int32, (384, 128), 0)
    oj = lax.broadcasted_iota(jnp.int32, (384, 128), 1)
    source = (oi & 15) * 24 + (oi >> 4) - oj
    order = [jnp.where(source == 128 * k, 1.0, 0.0).astype(BF16) for k in range(3)]
    order = jnp.concatenate(order, axis=1)

    loads[2].wait()
    loads[3].wait()
    for r in range(24):
        gt[:, tile(r)] = jnp.dot(gv[r], perm, preferred_element_type=F32).astype(BF16)

    for k in (3 - 2 * c, 1 + 2 * c, 2):
        v = (zh + k) % 4
        ref = cb.at[w * 4 + v]
        send(ref, ref, sa.at[2], ra.at[v], at_zh(1 + 2 * c), zl).wait_recv()
        if len(to_zh) == 2:
            to_zh.append(send(ref, ref, sa.at[2], ra.at[v], at_zh(1 + 2 * c), zl))
            to_zh[2].start()
        for copy in forward(v):
            copy.start()

    to_zl = [
        send(cp.at[zl], cp.at[zl], sp.at[k], rp.at[zl], p, (zl + k) % 8) for k in range(1, 8)
    ]
    for copy in to_zl:
        copy.start()

    for k in (1, 3, 2):
        for v in range(4):
            slot = ((w + k) % 4) * 4 + v
            ref = cb.at[slot]
            send(ref, ref, sb.at[v, k - 1], rb.at[slot], at_w(k), zl).wait_recv()

    group = cb[...].astype(F32).reshape(384, 384).astype(BF16)
    group = jnp.dot(order, group, preferred_element_type=F32)
    dd[c * 4 + a] = group.reshape(24, 16, 384).astype(BF16)

    mine_d = dd.at[c * 4 + a]
    to_a = [send(mine_d, mine_d, sc.at[k - 1], rc.at[a], at_a(k), zl) for k in range(1, 4)]
    for copy in to_a:
        copy.start()

    def to_core(v):
        ref = dd.at[c * 4 + v]
        return send(ref, ref, sd.at[v], rd.at[v], core_peer, zl)

    to_core(a).start()

    half16 = lax.broadcasted_iota(jnp.int32, (16, 128), 1) < 64
    plain = [jnp.where(half16, 2.0 * j + 1.0, 2.0 * j + 2.0).astype(BF16) for j in range(3)]
    swapped = [jnp.where(half16, 2.0 * j + 2.0, 2.0 * j + 1.0).astype(BF16) for j in range(3)]

    def expand(g):
        start = pl.multiple_of(g * 16, 16)

        @pl.loop(0, 24, step=4)
        def _(r0):
            val, val_r = [], []
            for u in range(4):
                val.append([dd[g, r0 + u, :, tile(j)] for j in range(3)])
                val_r.append([pltpu.roll(v.astype(F32), 64, 1).astype(BF16) for v in val[u]])
            for m in range(6):
                t = tm[pl.ds(start, 16), tile(m)]
                acc = [jnp.zeros((16, 128), BF16)] * 4
                for j in GROUPS[m]:
                    straight, crossed = t == plain[j], t == swapped[j]
                    for u in range(4):
                        acc[u] = jnp.where(straight, val[u][j], acc[u])
                        acc[u] = jnp.where(crossed, val_r[u][j], acc[u])
                for u in range(4):
                    at = pl.multiple_of((r0 + u) * 128 + g * 16, 16)
                    ee[pl.ds(at, 16), tile(m)] = acc[u]

    expand(c * 4 + a)

    for k in range(1, 8):
        v = (zl + k) % 8
        send(cp.at[v], cp.at[v], sp.at[k], rp.at[v], p, v).wait_recv()
    goal_p = [jnp.where(half24, 2.0 * j + 1.0, 2.0 * j + 2.0) for j in range(3)]
    goal_s = [jnp.where(half24, 2.0 * j + 2.0, 2.0 * j + 1.0) for j in range(3)]

    @pl.loop(0, 8)
    def _(q):
        val = [cp[q, :, tile(j)].astype(F32) for j in range(3)]
        val_r = [pltpu.roll(v, 64, 1) for v in val]
        for m in range(6):
            t = jnp.broadcast_to(tp[q, :, tile(m)], (24, 128))
            acc = jnp.zeros((24, 128), F32)
            for j in GROUPS[m]:
                acc = jnp.where(t == goal_p[j], val[j], acc)
                acc = jnp.where(t == goal_s[j], val_r[j], acc)
            mp[q, :, tile(m)] = acc

    for m in range(6):
        ft[m] = mp[:, :, tile(m)].reshape(192, 128).T.astype(BF16)

    other = y * (1 - c) + x * c

    def from_core(v):
        ref = dd.at[(1 - c) * 4 + v]
        send(ref, ref, sd.at[v], rd.at[v], core_peer, zl).wait_recv()
        expand((1 - c) * 4 + v)

    from_core(other)
    for k in (1, 3, 2):
        v = (a + k) % 4
        ref = dd.at[c * 4 + v]
        send(ref, ref, sc.at[k - 1], rc.at[v], at_a(k), zl).wait_recv()
        to_core(v).start()
        expand(c * 4 + v)
    for k in (1, 3, 2):
        from_core((other + k) % 4)

    @pl.loop(0, 3)
    def _(n):
        cols = pl.ds(pl.multiple_of(n * 256, 256), 256)
        got = jnp.dot(gt[...], ee[:, cols], preferred_element_type=F32)
        pt[:, :, cols] = got.reshape(8, 24, 256)

    def right(j):
        return send(rr.at[j], rr.at[j], s_r.at[j], r_r.at[j], p, (zl + 1) % 8)

    def left(j):
        return send(rl.at[j], rl.at[j], s_l.at[j], r_l.at[j], p, (zl + 7) % 8)

    def slot(s):
        @pl.when(zl <= s)
        def _():
            j = zl + 7 - s

            @pl.when(zl > 0)
            def _():
                right(j).wait_recv()
                rr[j] = rr[j] + pt[j]

            @pl.when(zl == 0)
            def _():
                rr[j] = pt[j]

            right(j).start()

        @pl.when(zl >= 7 - s)
        def _():
            j = zl - 7 + s

            @pl.when(zl < 7)
            def _():
                left(j).wait_recv()
                rl[j] = rl[j] + pt[j]

            @pl.when(zl == 7)
            def _():
                rl[j] = pt[j]

            left(j).start()

        if s >= 2:

            @pl.when(zl <= s - 2)
            def _():
                right(zl + 9 - s).wait_send()

            @pl.when(zl >= 9 - s)
            def _():
                left(zl - 9 + s).wait_send()

    slot(0)

    half128 = lax.broadcasted_iota(jnp.int32, (128, 128), 0) < 64
    for m in range(6):
        part = pt[:, :, tile(m)].reshape(192, 128)
        hi = part.astype(BF16)
        lo = (part - hi.astype(F32)).astype(BF16)
        both = jnp.dot(ft[m], hi, preferred_element_type=F32)
        both = both + jnp.dot(ft[m], lo, preferred_element_type=F32)
        both = jnp.where(half128, both, pltpu.roll(both, 64, 1)).T
        for v in range(8):
            sh[v * 3 + m // 2, :, tile(m % 2)] = both[v * 8 : v * 8 + 8]

    owner = d < 24

    def share_to(k):
        v = (d + k) % 24
        return send(sh.at[v], b1.at[d], s1.at[k], r1.at[d], in_plane(v), zl)

    def piece_to(k):
        return send(b6.at[d], b6.at[d], s6.at[k], r6.at[d], in_plane(d + k), zl)

    def to_line(k):
        return send(b3.at[zl], b3.at[zl], s3.at[k], r3.at[zl], p, (zl + k) % 8)

    def to_pair():
        peer = prow_of(x, zh + 1 - 2 * (zh % 2), y, c)
        return send(b4.at[0], b4.at[1], s4.at[0], r4.at[0], peer, zl)

    def to_other_pair():
        return send(b4.at[2], b4.at[3], s4.at[1], r4.at[1], prow_of(x, 3 - zh, y, c), zl)

    def total(ref, n):
        parts = [ref[v] for v in range(n)]
        while len(parts) > 1:
            parts = [u + v for u, v in zip(parts[::2], parts[1::2])]
        return parts[0]

    def phase1():
        @pl.when(d >= 24)
        def _():
            share_to(0).start()

        for k in range(1, 24):
            share_to(k).start()

    def phase2():
        @pl.when(owner)
        def _():
            b1[d] = sh[d]
            for k in range(1, 32):
                v = (d + k) % 32
                send(b1.at[v], b1.at[v], s1.at[0], r1.at[v], in_plane(v), zl).wait_recv()
            b3[zl] = total(b1, 32)
            for k in range(1, 8):
                to_line(k).start()

    def phase3():
        @pl.when(owner)
        def _():
            for k in range(1, 8):
                v = (zl + k) % 8
                send(b3.at[v], b3.at[v], s3.at[k], r3.at[v], p, v).wait_recv()
            b4[0] = total(b3, 8)
            to_pair().start()

    def phase3b():
        @pl.when(owner)
        def _():
            to_pair().wait_recv()
            b4[2] = b4[0] + b4[1]
            to_other_pair().start()

    def phase4():
        @pl.when(owner)
        def _():
            to_other_pair().wait_recv()
            b6[d] = b4[2] + b4[3]
            for k in range(1, 32):
                piece_to(k).start()

    def phase5():
        for v in range(24):

            @pl.when(d != v)
            def _():
                home = prow_of(v // 8, zh, (v // 2) % 4, v % 2)
                send(b6.at[v], b6.at[v], s6.at[0], r6.at[v], home, zl).wait_recv()

        for v in range(24):
            rows, cols = slice(v // 3 * 8, v // 3 * 8 + 8), slice(v % 3 * 256, v % 3 * 256 + 256)
            diag_ref[rows, cols] = dinv_ref[rows, cols] - b6[v]

    phase1()
    slot(1)
    slot(2)
    phase2()
    slot(3)
    slot(4)
    phase3()
    slot(5)
    phase3b()
    slot(6)

    off_ref[...] = pt[zl]

    @pl.when(zl > 0)
    def _():
        right(zl).wait_recv()
        off_ref[...] += rr[zl]

    @pl.when(zl < 7)
    def _():
        left(zl).wait_recv()
        off_ref[...] += rl[zl]

    phase4()
    phase5()

    for copy in to_zh:
        copy.wait_send()
    for v in range(4):
        for copy in forward(v):
            copy.wait_send()
    for copy in to_zl:
        copy.wait_send()
    for copy in to_a:
        copy.wait_send()
    for v in range(4):
        to_core(v).wait_send()
    for s in (5, 6):

        @pl.when(zl <= s)
        def _():
            right(zl + 7 - s).wait_send()

        @pl.when(zl >= 7 - s)
        def _():
            left(zl - 7 + s).wait_send()

    @pl.when(d >= 24)
    def _():
        share_to(0).wait_send()

    for k in range(1, 24):
        share_to(k).wait_send()

    @pl.when(owner)
    def _():
        for k in range(1, 8):
            to_line(k).wait_send()
        to_pair().wait_send()
        to_other_pair().wait_send()
        for k in range(1, 32):
            piece_to(k).wait_send()


def body(ainv_sep, lower_blocks, pattern, diag_inv):
    dma = pltpu.SemaphoreType.DMA
    vmem = pltpu.VMEM
    off, diag = pl.pallas_call(
        kernel,
        out_shape=(
            jax.ShapeDtypeStruct((24, 768), F32),
            jax.ShapeDtypeStruct((64, 768), F32),
        ),
        in_specs=[pl.BlockSpec(memory_space=pl.ANY)] * 4,
        out_specs=(pl.BlockSpec(memory_space=vmem), pl.BlockSpec(memory_space=vmem)),
        scratch_shapes=[
            vmem((12, 1024), jnp.int32),
            vmem((24, 768), BF16),
            vmem((64, 768), F32),
            vmem((16, 24, 384), BF16),
            vmem((8, 24, 16, 384), BF16),
            vmem((8, 24, 384), BF16),
            vmem((24, 192, 128), BF16),
            vmem((192, 3072), BF16),
            vmem((128, 768), BF16),
            vmem((8, 1, 768), F32),
            vmem((3072, 768), BF16),
            vmem((8, 24, 768), F32),
            vmem((6, 128, 192), BF16),
            vmem((8, 24, 768), F32),
            vmem((8, 24, 768), F32),
            vmem((8, 24, 768), F32),
            vmem((24, 8, 256), F32),
            vmem((32, 8, 256), F32),
            vmem((8, 8, 256), F32),
            vmem((4, 8, 256), F32),
            vmem((24, 8, 256), F32),
            dma((4,)),
            dma((3,)), dma((4,)),
            dma((4, 3)), dma((16,)),
            dma((3,)), dma((4,)),
            dma((4,)), dma((4,)),
            dma((8,)), dma((8,)),
            dma((8,)), dma((8,)),
            dma((8,)), dma((8,)),
            dma((24,)), dma((32,)),
            dma((8,)), dma((8,)),
            dma((2,)), dma((2,)),
            dma((32,)), dma((24,)),
        ],
        compiler_params=pltpu.CompilerParams(
            collective_id=0, has_side_effects=True, vmem_limit_bytes=60 * 1024 * 1024
        ),
    )(
        pattern.T,
        lower_blocks,
        diag_inv.T,
        ainv_sep.transpose(1, 2, 3, 0).reshape(24, 192, 128),
    )
    return off, diag.T


def solution(mesh):
    return jax.shard_map(
        body,
        mesh=mesh,
        in_specs=(P(None, "pcol", None, "prow"), P(("prow", "pcol"), None), P(), P()),
        out_specs=(P(("prow", "pcol"), None), P()),
        check_vma=False,
    )
```

time: 188 us -> 102 us (0.54)
  Pallas kernels: 182 us -> 98.1 us
  local copies, waits for them, and re-layouts: 5.11 us -> 3.14 us
    pallas_call x1, Pallas kernels: 182 us -> 98.1 us  [body(): pl.pallas_call(kernel, out_shape=(jax.ShapeDtypeStruct((24, 768), F32), j...]
    unnamed x10 -> x2, local copies, waits for them, and re-layouts: 5.11 us -> 3.14 us
where the time goes in v2:
time: 102 us
  Pallas kernels  98.1 us (96%)
  local copies, waits for them, and re-layouts  3.14 us (3%)
    pallas_call x1, Pallas kernels, body(): pl.pallas_call(kernel, out_shape=(jax.ShapeDtypeStruct((24, 768), F32), j...  98.1 us
    unnamed x2, local copies, waits for them, and re-layouts  3.14 us

profile of v2, /device:TPU:1, one launch (start us, length us, event | category | flops | bytes accessed | tf_op | source)
XLA Modules:
  0.0 101.8 jit_solution(7394467874177197682)
XLA Ops:
  0.6 98.1 %shard_map.59 = (f32[24,768]{1,0:T(8,128)}, f32[64,768]{1,0:T(8,128)}) custom-call(s32[12,1024]{1,0:T(8,128)} %bitcast.9, bf16[24,768]{1,0:T(8,128)(2,1)} %low_hbm.1, f32[64,768]{1,0:T(8,128)} %bitcast.8, bf16[24,192,128]{2,1,0:T(8,128)(2,1)} %bitcast.6), custom_call_target="tpu_custom_call" | custom-call | tf_op jit(solution)/shard_map/pallas_call | solution.py:467
  98.7 1.5 %copy.8 = f32[24,768]{1,0:T(8,128)} copy(f32[24,768]{1,0:T(8,128)} %get-tuple-element.8) | data formatting | bytes 147456
  100.2 1.6 %copy.9 = f32[768,64]{0,1:T(8,128)} copy(f32[768,64]{0,1:T(8,128)} %bitcast.7) | data formatting | bytes 393216

commit v3 on v2

--- a/solution.py
+++ b/solution.py
@@ -21,7 +21,7 @@
 
 
 def place(i):
-    c, a, w, zh = i >> 6, (i >> 4) & 3, (i >> 2) & 3, i & 3
+    c, zh, a, w = i >> 6, (i >> 4) & 3, (i >> 2) & 3, i & 3
     x = jnp.where(c == 0, a, w)
     y = jnp.where(c == 0, w, a)
     return (x << 5) + (zh << 3) + (y << 1) + c
@@ -107,7 +107,7 @@
             tp[q, :, tile(m)] = t[128 + q : 129 + q]
 
     half24 = lax.broadcasted_iota(jnp.int32, (24, 128), 1) < 64
-    own = cb.at[w * 4 + zh]
+    own = cb.at[zh, a, w]
     mine = tp[zl]
     parts = [None] * 3
     for m in range(6):
@@ -124,16 +124,47 @@
 
     pl.semaphore_wait(barrier, 40)
 
+    below, above, far = (zh + 3 - 2 * c) % 4, (zh + 1 + 2 * c) % 4, (zh + 2) % 4
+
+    def along_w(v):
+        ref = cb.at[v, a, w]
+        return [send(ref, ref, sb.at[v, k - 1], rb.at[v, w], at_w(k), zl) for k in range(1, 4)]
+
+    def got_w(v):
+        for k in (1, 3, 2):
+            u = (w + k) % 4
+            ref = cb.at[v, a, u]
+            send(ref, ref, sb.at[v, 0], rb.at[v, u], at_w(k), zl).wait_recv()
+
+    def along_a(v):
+        ref = cb.at[v, a]
+        return [send(ref, ref, sc.at[v, k - 1], rc.at[v, a], at_a(k), zl) for k in range(1, 4)]
+
+    def got_a(v):
+        for k in (1, 3, 2):
+            u = (a + k) % 4
+            ref = cb.at[v, u]
+            send(ref, ref, sc.at[v, 0], rc.at[v, u], at_a(k), zl).wait_recv()
+
+    def to_core(v):
+        ref = dd.at[c * 4 + v]
+        return send(ref, ref, sd.at[v], rd.at[v], core_peer, zl)
+
+    def handed_on():
+        ref = cb.at[below, a, w]
+        return send(ref, ref, sa.at[2], ra.at[below], at_zh(1 + 2 * c), zl)
+
+    def got_zh(v):
+        ref = cb.at[v, a, w]
+        send(ref, ref, sa.at[0], ra.at[v], at_zh(1), zl).wait_recv()
+
+    def begin(copies):
+        for copy in copies:
+            copy.start()
+
     to_zh = [send(own, own, sa.at[k // 2], ra.at[zh], at_zh(k), zl) for k in (1, 3)]
-    for copy in to_zh:
-        copy.start()
-
-    def forward(v):
-        ref = cb.at[w * 4 + v]
-        return [send(ref, ref, sb.at[v, k - 1], rb.at[w * 4 + v], at_w(k), zl) for k in range(1, 4)]
-
-    for copy in forward(zh):
-        copy.start()
+    begin(to_zh)
+    begin(along_w(zh))
 
     gi = lax.broadcasted_iota(jnp.int32, (128, 128), 0)
     gj = lax.broadcasted_iota(jnp.int32, (128, 128), 1)
@@ -148,43 +179,6 @@
     loads[3].wait()
     for r in range(24):
         gt[:, tile(r)] = jnp.dot(gv[r], perm, preferred_element_type=F32).astype(BF16)
-
-    for k in (3 - 2 * c, 1 + 2 * c, 2):
-        v = (zh + k) % 4
-        ref = cb.at[w * 4 + v]
-        send(ref, ref, sa.at[2], ra.at[v], at_zh(1 + 2 * c), zl).wait_recv()
-        if len(to_zh) == 2:
-            to_zh.append(send(ref, ref, sa.at[2], ra.at[v], at_zh(1 + 2 * c), zl))
-            to_zh[2].start()
-        for copy in forward(v):
-            copy.start()
-
-    to_zl = [
-        send(cp.at[zl], cp.at[zl], sp.at[k], rp.at[zl], p, (zl + k) % 8) for k in range(1, 8)
-    ]
-    for copy in to_zl:
-        copy.start()
-
-    for k in (1, 3, 2):
-        for v in range(4):
-            slot = ((w + k) % 4) * 4 + v
-            ref = cb.at[slot]
-            send(ref, ref, sb.at[v, k - 1], rb.at[slot], at_w(k), zl).wait_recv()
-
-    group = cb[...].astype(F32).reshape(384, 384).astype(BF16)
-    group = jnp.dot(order, group, preferred_element_type=F32)
-    dd[c * 4 + a] = group.reshape(24, 16, 384).astype(BF16)
-
-    mine_d = dd.at[c * 4 + a]
-    to_a = [send(mine_d, mine_d, sc.at[k - 1], rc.at[a], at_a(k), zl) for k in range(1, 4)]
-    for copy in to_a:
-        copy.start()
-
-    def to_core(v):
-        ref = dd.at[c * 4 + v]
-        return send(ref, ref, sd.at[v], rd.at[v], core_peer, zl)
-
-    to_core(a).start()
 
     half16 = lax.broadcasted_iota(jnp.int32, (16, 128), 1) < 64
     plain = [jnp.where(half16, 2.0 * j + 1.0, 2.0 * j + 2.0).astype(BF16) for j in range(3)]
@@ -211,45 +205,76 @@
                     at = pl.multiple_of((r0 + u) * 128 + g * 16, 16)
                     ee[pl.ds(at, 16), tile(m)] = acc[u]
 
-    expand(c * 4 + a)
-
-    for k in range(1, 8):
-        v = (zl + k) % 8
-        send(cp.at[v], cp.at[v], sp.at[k], rp.at[v], p, v).wait_recv()
     goal_p = [jnp.where(half24, 2.0 * j + 1.0, 2.0 * j + 2.0) for j in range(3)]
     goal_s = [jnp.where(half24, 2.0 * j + 2.0, 2.0 * j + 1.0) for j in range(3)]
 
-    @pl.loop(0, 8)
-    def _(q):
-        val = [cp[q, :, tile(j)].astype(F32) for j in range(3)]
-        val_r = [pltpu.roll(v, 64, 1) for v in val]
+    def line_rows():
+        @pl.loop(0, 8)
+        def _(q):
+            val = [cp[q, :, tile(j)].astype(F32) for j in range(3)]
+            val_r = [pltpu.roll(v, 64, 1) for v in val]
+            for m in range(6):
+                t = jnp.broadcast_to(tp[q, :, tile(m)], (24, 128))
+                acc = jnp.zeros((24, 128), F32)
+                for j in GROUPS[m]:
+                    acc = jnp.where(t == goal_p[j], val[j], acc)
+                    acc = jnp.where(t == goal_s[j], val_r[j], acc)
+                mp[q, :, tile(m)] = acc
+
         for m in range(6):
-            t = jnp.broadcast_to(tp[q, :, tile(m)], (24, 128))
-            acc = jnp.zeros((24, 128), F32)
-            for j in GROUPS[m]:
-                acc = jnp.where(t == goal_p[j], val[j], acc)
-                acc = jnp.where(t == goal_s[j], val_r[j], acc)
-            mp[q, :, tile(m)] = acc
-
-    for m in range(6):
-        ft[m] = mp[:, :, tile(m)].reshape(192, 128).T.astype(BF16)
-
-    other = y * (1 - c) + x * c
+            ft[m] = mp[:, :, tile(m)].reshape(192, 128).T.astype(BF16)
+
+    def regroup(v):
+        group = cb[v].astype(F32).reshape(384, 384).astype(BF16)
+        group = jnp.dot(order, group, preferred_element_type=F32)
+        dd[c * 4 + v] = group.reshape(24, 16, 384).astype(BF16)
+        to_core(v).start()
 
     def from_core(v):
         ref = dd.at[(1 - c) * 4 + v]
         send(ref, ref, sd.at[v], rd.at[v], core_peer, zl).wait_recv()
         expand((1 - c) * 4 + v)
 
-    from_core(other)
-    for k in (1, 3, 2):
-        v = (a + k) % 4
-        ref = dd.at[c * 4 + v]
-        send(ref, ref, sc.at[k - 1], rc.at[v], at_a(k), zl).wait_recv()
-        to_core(v).start()
-        expand(c * 4 + v)
-    for k in (1, 3, 2):
-        from_core((other + k) % 4)
+    to_zl = [
+        send(cp.at[zl], cp.at[zl], sp.at[k], rp.at[zl], p, (zl + k) % 8) for k in range(1, 8)
+    ]
+
+    got_w(zh)
+    begin(along_a(zh))
+    got_zh(below)
+    handed_on().start()
+    begin(along_w(below))
+    got_zh(above)
+    begin(along_w(above))
+    begin(to_zl)
+    got_a(zh)
+    regroup(zh)
+    expand(c * 4 + zh)
+    got_w(below)
+    begin(along_a(below))
+    got_w(above)
+    begin(along_a(above))
+    got_zh(far)
+    begin(along_w(far))
+    from_core(zh)
+    got_a(below)
+    regroup(below)
+    got_a(above)
+    regroup(above)
+    got_w(far)
+    begin(along_a(far))
+    expand(c * 4 + below)
+    expand(c * 4 + above)
+    from_core(below)
+    from_core(above)
+    for k in range(1, 8):
+        v = (zl + k) % 8
+        send(cp.at[v], cp.at[v], sp.at[k], rp.at[v], p, v).wait_recv()
+    line_rows()
+    got_a(far)
+    regroup(far)
+    expand(c * 4 + far)
+    from_core(far)
 
     @pl.loop(0, 3)
     def _(n):
@@ -423,16 +448,12 @@
     phase4()
     phase5()
 
-    for copy in to_zh:
+    for copy in to_zh + to_zl:
         copy.wait_send()
+    handed_on().wait_send()
     for v in range(4):
-        for copy in forward(v):
+        for copy in along_w(v) + along_a(v):
             copy.wait_send()
-    for copy in to_zl:
-        copy.wait_send()
-    for copy in to_a:
-        copy.wait_send()
-    for v in range(4):
         to_core(v).wait_send()
     for s in (5, 6):
 
@@ -476,7 +497,7 @@
             vmem((12, 1024), jnp.int32),
             vmem((24, 768), BF16),
             vmem((64, 768), F32),
-            vmem((16, 24, 384), BF16),
+            vmem((4, 4, 4, 24, 384), BF16),
             vmem((8, 24, 16, 384), BF16),
             vmem((8, 24, 384), BF16),
             vmem((24, 192, 128), BF16),
@@ -496,8 +517,8 @@
             vmem((24, 8, 256), F32),
             dma((4,)),
             dma((3,)), dma((4,)),
-            dma((4, 3)), dma((16,)),
-            dma((3,)), dma((4,)),
+            dma((4, 3)), dma((4, 4)),
+            dma((4, 3)), dma((4, 4)),
             dma((4,)), dma((4,)),
             dma((8,)), dma((8,)),
             dma((8,)), dma((8,)),

time: 102 us -> 94.7 us (0.928)
  Pallas kernels: 98.1 us -> 90.6 us
    pallas_call x1, Pallas kernels: 98.1 us -> 90.6 us  [body(): pl.pallas_call(kernel, out_shape=(jax.ShapeDtypeStruct((24, 768), F32), j...]
where the time goes in v3:
time: 94.7 us; the launch traced here: 94.4 us
  Pallas kernels  90.6 us (96%)
  local copies, waits for them, and re-layouts  3.14 us (3%)
    pallas_call x1, Pallas kernels, body(): pl.pallas_call(kernel, out_shape=(jax.ShapeDtypeStruct((24, 768), F32), j...  90.6 us
    unnamed x2, local copies, waits for them, and re-layouts  3.14 us

profile of v3, /device:TPU:1, one launch (start us, length us, event | category | flops | bytes accessed | tf_op | source)
XLA Modules:
  0.0 94.4 jit_solution(3296881758023043718)
XLA Ops:
  0.6 90.6 %shard_map.59 = (f32[24,768]{1,0:T(8,128)}, f32[64,768]{1,0:T(8,128)}) custom-call(s32[12,1024]{1,0:T(8,128)} %bitcast.9, bf16[24,768]{1,0:T(8,128)(2,1)} %low_hbm.1, f32[64,768]{1,0:T(8,128)} %bitcast.8, bf16[24,192,128]{2,1,0:T(8,128)(2,1)} %bitcast.6), custom_call_target="tpu_custom_call" | custom-call | tf_op jit(solution)/shard_map/pallas_call | solution.py:488
  91.3 1.5 %copy.8 = f32[24,768]{1,0:T(8,128)} copy(f32[24,768]{1,0:T(8,128)} %get-tuple-element.8) | data formatting | bytes 147456
  92.8 1.6 %copy.9 = f32[768,64]{0,1:T(8,128)} copy(f32[768,64]{0,1:T(8,128)} %bitcast.7) | data formatting | bytes 393216

commit v4 on v3

--- a/solution.py
+++ b/solution.py
@@ -44,7 +44,7 @@
 def kernel(
     pat_hbm, low_hbm, dinv_hbm, g_hbm, off_ref, diag_ref,
     pat_ref, low_ref, dinv_ref, cb, dd, cp, gv, gt, tm, tp, ee, mp, ft, pt, rr, rl, sh, b1, b3, b4, b6,
-    isem, sa, ra, sb, rb, sc, rc, sd, rd, sp, rp, s_r, r_r, s_l, r_l,
+    isem, sa, ra, sb, rb, sc, rc, sf, rf, sd, rd, sp, rp, s_r, r_r, s_l, r_l,
     s1, r1, s3, r3, s4, r4, s6, r6,
 ):
     p = lax.axis_index("prow")
@@ -93,18 +93,20 @@
     loads[1].wait()
 
     slots = slot_rows(pat_ref[...].astype(F32)).astype(BF16)
-    row = lax.broadcasted_iota(jnp.int32, (144, 128), 0)
-    lane = lax.broadcasted_iota(jnp.int32, (144, 128), 1)
-    wanted = jnp.where(row < 128, (place(row & 127) << 3) + zl, p * 8 + (row & 7)) - lane
-    pick = [jnp.where(wanted == 128 * k, 1.0, 0.0).astype(BF16) for k in range(8)]
-    pick = jnp.concatenate(pick, axis=1)
-    table = lax.dot_general(pick, slots, (((1,), (1,)), ((), ())), preferred_element_type=F32)
-    low_half = lane < 64
-    for m in range(6):
-        t = jnp.where(low_half, table[:, 2 * m : 2 * m + 1], table[:, 2 * m + 1 : 2 * m + 2])
-        tm[:, tile(m)] = t[:128].astype(BF16)
+    def slots_of(rows, wanted):
+        lane = lax.broadcasted_iota(jnp.int32, (rows, 128), 1)
+        pick = [jnp.where(wanted - lane == 128 * k, 1.0, 0.0).astype(BF16) for k in range(8)]
+        table = lax.dot_general(
+            jnp.concatenate(pick, axis=1), slots, (((1,), (1,)), ((), ())), preferred_element_type=F32
+        )
+        return [
+            jnp.where(lane < 64, table[:, 2 * m : 2 * m + 1], table[:, 2 * m + 1 : 2 * m + 2])
+            for m in range(6)
+        ]
+
+    for m, t in enumerate(slots_of(8, p * 8 + lax.broadcasted_iota(jnp.int32, (8, 128), 0))):
         for q in range(8):
-            tp[q, :, tile(m)] = t[128 + q : 129 + q]
+            tp[q, :, tile(m)] = t[q : q + 1]
 
     half24 = lax.broadcasted_iota(jnp.int32, (24, 128), 1) < 64
     own = cb.at[zh, a, w]
@@ -146,6 +148,24 @@
             ref = cb.at[v, u]
             send(ref, ref, sc.at[v, 0], rc.at[v, u], at_a(k), zl).wait_recv()
 
+    def plane_at(ka, kw):
+        u, v = (a + ka) % 4, (w + kw) % 4
+        return prow_of(u * (1 - c) + v * c, zh, v * (1 - c) + u * c, c)
+
+    others = [(ka, kw) for ka in (0, 1, 3, 2) for kw in (0, 1, 3, 2)][1:]
+
+    def spread(v):
+        ref = cb.at[v, a, w]
+        return [
+            send(ref, ref, sf.at[ka, kw], rf.at[a, w], plane_at(ka, kw), zl) for ka, kw in others
+        ]
+
+    def got_spread(v):
+        for ka, kw in others:
+            u, t = (a + ka) % 4, (w + kw) % 4
+            ref = cb.at[v, u, t]
+            send(ref, ref, sf.at[ka, kw], rf.at[u, t], plane_at(ka, kw), zl).wait_recv()
+
     def to_core(v):
         ref = dd.at[c * 4 + v]
         return send(ref, ref, sd.at[v], rd.at[v], core_peer, zl)
@@ -165,20 +185,6 @@
     to_zh = [send(own, own, sa.at[k // 2], ra.at[zh], at_zh(k), zl) for k in (1, 3)]
     begin(to_zh)
     begin(along_w(zh))
-
-    gi = lax.broadcasted_iota(jnp.int32, (128, 128), 0)
-    gj = lax.broadcasted_iota(jnp.int32, (128, 128), 1)
-    perm = jnp.where(gi == place(gj), -1.0, 0.0).astype(BF16)
-    oi = lax.broadcasted_iota(jnp.int32, (384, 128), 0)
-    oj = lax.broadcasted_iota(jnp.int32, (384, 128), 1)
-    source = (oi & 15) * 24 + (oi >> 4) - oj
-    order = [jnp.where(source == 128 * k, 1.0, 0.0).astype(BF16) for k in range(3)]
-    order = jnp.concatenate(order, axis=1)
-
-    loads[2].wait()
-    loads[3].wait()
-    for r in range(24):
-        gt[:, tile(r)] = jnp.dot(gv[r], perm, preferred_element_type=F32).astype(BF16)
 
     half16 = lax.broadcasted_iota(jnp.int32, (16, 128), 1) < 64
     plain = [jnp.where(half16, 2.0 * j + 1.0, 2.0 * j + 2.0).astype(BF16) for j in range(3)]
@@ -247,6 +253,23 @@
     got_zh(above)
     begin(along_w(above))
     begin(to_zl)
+    row = lax.broadcasted_iota(jnp.int32, (128, 128), 0)
+    for m, t in enumerate(slots_of(128, (place(row) << 3) + zl)):
+        tm[:, tile(m)] = t.astype(BF16)
+    gi = lax.broadcasted_iota(jnp.int32, (128, 128), 0)
+    gj = lax.broadcasted_iota(jnp.int32, (128, 128), 1)
+    perm = jnp.where(gi == place(gj), -1.0, 0.0).astype(BF16)
+    oi = lax.broadcasted_iota(jnp.int32, (384, 128), 0)
+    oj = lax.broadcasted_iota(jnp.int32, (384, 128), 1)
+    source = (oi & 15) * 24 + (oi >> 4) - oj
+    order = [jnp.where(source == 128 * k, 1.0, 0.0).astype(BF16) for k in range(3)]
+    order = jnp.concatenate(order, axis=1)
+
+    loads[2].wait()
+    loads[3].wait()
+    for r in range(24):
+        gt[:, tile(r)] = jnp.dot(gv[r], perm, preferred_element_type=F32).astype(BF16)
+
     got_a(zh)
     regroup(zh)
     expand(c * 4 + zh)
@@ -255,23 +278,17 @@
     got_w(above)
     begin(along_a(above))
     got_zh(far)
-    begin(along_w(far))
+    begin(spread(far))
     from_core(zh)
     got_a(below)
     regroup(below)
     got_a(above)
     regroup(above)
-    got_w(far)
-    begin(along_a(far))
     expand(c * 4 + below)
     expand(c * 4 + above)
     from_core(below)
     from_core(above)
-    for k in range(1, 8):
-        v = (zl + k) % 8
-        send(cp.at[v], cp.at[v], sp.at[k], rp.at[v], p, v).wait_recv()
-    line_rows()
-    got_a(far)
+    got_spread(far)
     regroup(far)
     expand(c * 4 + far)
     from_core(far)
@@ -330,6 +347,10 @@
                 left(zl - 9 + s).wait_send()
 
     slot(0)
+    for k in range(1, 8):
+        v = (zl + k) % 8
+        send(cp.at[v], cp.at[v], sp.at[k], rp.at[v], p, v).wait_recv()
+    line_rows()
 
     half128 = lax.broadcasted_iota(jnp.int32, (128, 128), 0) < 64
     for m in range(6):
@@ -451,9 +472,12 @@
     for copy in to_zh + to_zl:
         copy.wait_send()
     handed_on().wait_send()
-    for v in range(4):
+    for v in (zh, below, above):
         for copy in along_w(v) + along_a(v):
             copy.wait_send()
+    for copy in spread(far):
+        copy.wait_send()
+    for v in range(4):
         to_core(v).wait_send()
     for s in (5, 6):
 
@@ -519,6 +543,7 @@
             dma((3,)), dma((4,)),
             dma((4, 3)), dma((4, 4)),
             dma((4, 3)), dma((4, 4)),
+            dma((4, 4)), dma((4, 4)),
             dma((4,)), dma((4,)),
             dma((8,)), dma((8,)),
             dma((8,)), dma((8,)),

time: 94.7 us -> 93.8 us (level)
  no operation moved by 1% of the time
where the time goes in v4:
time: 93.8 us; the launch traced here: 93.5 us
  Pallas kernels  89.7 us (96%)
  local copies, waits for them, and re-layouts  3.14 us (3%)
    pallas_call x1, Pallas kernels, body(): pl.pallas_call(kernel, out_shape=(jax.ShapeDtypeStruct((24, 768), F32), j...  89.7 us
    unnamed x2, local copies, waits for them, and re-layouts  3.14 us

profile of v4, /device:TPU:1, one launch (start us, length us, event | category | flops | bytes accessed | tf_op | source)
XLA Modules:
  0.0 93.5 jit_solution(16708580548382072181)
XLA Ops:
  0.6 89.7 %shard_map.59 = (f32[24,768]{1,0:T(8,128)}, f32[64,768]{1,0:T(8,128)}) custom-call(s32[12,1024]{1,0:T(8,128)} %bitcast.9, bf16[24,768]{1,0:T(8,128)(2,1)} %low_hbm.1, f32[64,768]{1,0:T(8,128)} %bitcast.8, bf16[24,192,128]{2,1,0:T(8,128)(2,1)} %bitcast.6), custom_call_target="tpu_custom_call" | custom-call | tf_op jit(solution)/shard_map/pallas_call | solution.py:512
  90.4 1.5 %copy.8 = f32[24,768]{1,0:T(8,128)} copy(f32[24,768]{1,0:T(8,128)} %get-tuple-element.8) | data formatting | bytes 147456
  91.9 1.6 %copy.9 = f32[768,64]{0,1:T(8,128)} copy(f32[768,64]{0,1:T(8,128)} %bitcast.7) | data formatting | bytes 393216
